TPU v7x, 32 devices: a whole 2x2x4 slice. The times are simulated.
32 devices in a mesh: row: 8 (over z, x), col: 4 (over y, core).
Axes of the slice: x: 2, y: 2, z: 4, core: 2. Of those that a mesh axis runs over, the one named last changes fastest.
Arguments:
- cov: float32 [16384, 16384], P('row', 'col'), as said below
- noise: float32 [16384, 16384], P('row', 'col'), as said below
- diffusivity: float32 [128, 128], P('row'), may hold values from 0.25 to 1
- wind_x: float32 [128, 128], P('row'), may hold values from -1 to 1
- wind_y: float32 [128, 128], P('row'), may hold values from -1 to 1
Outputs:
- cov_next: float32 [16384, 16384], P('row', 'col')
Inputs may be any that keep to these rules, and one draw needn't show every extreme that they name: cov is symmetric. noise is symmetric.
All inputs are finite; a program needn't handle non-finite values.
Results may differ from a plain program's by a relative error of at most 0.00002.
Values sent between devices are 32-bit elements; how exact they have to be, the bound alone decides.
A program may use at most 384 MiB of HBM per device.

v0:
```python
import jax
import jax.numpy as jnp
from jax import lax
from jax.sharding import PartitionSpec as P

OFFSETS = ((0, 0), (1, 0), (-1, 0), (0, 1), (0, -1), (1, 1), (1, -1), (-1, 1), (-1, -1))
time_step = 0.1


def padded_2(cells, sides, width):
    for axis, dim in sides:
        count = lax.axis_size(axis)
        ends = count - 1
        head = lax.slice_in_dim(cells, 0, width, axis=dim)
        tail = lax.slice_in_dim(cells, cells.shape[dim] - width, cells.shape[dim], axis=dim)
        cells = jnp.concatenate(
            [
                lax.ppermute(tail, axis, [(i, (i + 1) % count) for i in range(ends)]),
                cells,
                lax.ppermute(head, axis, [((i + 1) % count, i) for i in range(ends)]),
            ],
            axis=dim,
        )
    return cells


def stencil_weights(kappa, flow_x, flow_y):
    edge = 4.0 / 6.0 * kappa
    corner = kappa / 6.0
    return jnp.stack(
        [
            -20.0 / 6.0 * kappa,
            edge - 0.5 * flow_x,
            edge + 0.5 * flow_x,
            edge - 0.5 * flow_y,
            edge + 0.5 * flow_y,
            corner,
            corner,
            corner,
            corner,
        ]
    )


def row_term(padded, weights):
    count = weights.shape[1]
    side = weights.shape[2]
    wide = jnp.pad(padded, ((0, 0), (1, 1), (0, 0)))
    total = jnp.zeros((count, side, padded.shape[2]), jnp.float32)
    for index, (step_x, step_y) in enumerate(OFFSETS):
        piece = wide[1 + step_x : 1 + step_x + count, 1 + step_y : 1 + step_y + side, :]
        total = total + weights[index][:, :, None] * piece
    return total


def col_term(padded, weights):
    count = weights.shape[1]
    side = weights.shape[2]
    wide = jnp.pad(padded, ((0, 0), (0, 0), (1, 1)))
    total = jnp.zeros((padded.shape[0], count, side), jnp.float32)
    for index, (step_x, step_y) in enumerate(OFFSETS):
        piece = wide[:, 1 + step_x : 1 + step_x + count, 1 + step_y : 1 + step_y + side]
        total = total + weights[index][None, :, :] * piece
    return total


def derive(padded, noise, row_weights, col_weights, side):
    rows = padded.shape[0] - 2 * side
    cols = padded.shape[1] - 2 * side
    middle_cols = padded[:, side : side + cols].reshape(rows // side + 2, side, cols)
    middle_rows = padded[side : side + rows, :].reshape(rows, cols // side + 2, side)
    along_rows = row_term(middle_cols, row_weights).reshape(rows, cols)
    along_cols = col_term(middle_rows, col_weights).reshape(rows, cols)
    return along_rows + along_cols + noise


def per_device(cov, noise, diffusivity, wind_x, wind_y):
    kappa, flow_x, flow_y = (
        lax.all_gather(diffusivity, "row", axis=0, tiled=True),
        lax.all_gather(wind_x, "row", axis=0, tiled=True),
        lax.all_gather(wind_y, "row", axis=0, tiled=True),
    )
    weights = stencil_weights(kappa, flow_x, flow_y)
    side = weights.shape[2]
    framed = jnp.pad(weights, ((0, 0), (1, 1), (0, 0)))
    row_count = cov.shape[0] // side
    col_count = cov.shape[1] // side
    row_start = lax.axis_index("row") * row_count
    col_start = lax.axis_index("col") * col_count
    row_wide = lax.dynamic_slice_in_dim(framed, row_start, row_count + 2, 1)
    col_wide = lax.dynamic_slice_in_dim(framed, col_start, col_count + 2, 1)
    row_inner = row_wide[:, 1:-1]
    col_inner = col_wide[:, 1:-1]

    def advance(field):
        padded = padded_2(field, (("row", 0), ("col", 1)), side)
        return derive(padded, noise, row_inner, col_inner, side)

    first = advance(cov)
    middle = cov + time_step * first
    second = advance(middle)
    return cov + 0.5 * time_step * (first + second)


def solution(mesh):
    return jax.shard_map(
        per_device,
        mesh=mesh,
        in_specs=(P("row", "col"), P("row", "col"), P("row", None), P("row", None), P("row", None)),
        out_specs=P("row", "col"),
        check_vma=False,
    )
```

profile of v0, /device:TPU:9, one launch (start us, length us, event | category | flops | bytes accessed | tf_op | source)
XLA Modules:
  0.0 1216.6 jit_solution(7583823941724923852)
XLA Ops:
  0.0 4.7 fusion.72
  10.9 105.4 %all_gather.9 = f32[128,128]{1,0:T(8,128)S(1)} all-gather(f32[16,128]{1,0:T(8,128)} %param.7), channel_id=1, replica_groups=mesh['row'=8,'col'=4] {'row'}, dimensions={0}, use_global_device_ids=true | all-gather | bytes 73728 | tf_op jit(solution)/shard_map/all_gather | solution.py:79
  116.3 24.3 %all_gather.10 = f32[128,128]{1,0:T(8,128)S(1)} all-gather(f32[16,128]{1,0:T(8,128)} %param.8), channel_id=1, replica_groups=mesh['row'=8,'col'=4] {'row'}, dimensions={0}, use_global_device_ids=true | all-gather | bytes 73728 | tf_op jit(solution)/shard_map/all_gather | solution.py:80
  140.7 24.3 %all_gather.11 = f32[128,128]{1,0:T(8,128)S(1)} all-gather(f32[16,128]{1,0:T(8,128)} %param.9), channel_id=1, replica_groups=mesh['row'=8,'col'=4] {'row'}, dimensions={0}, use_global_device_ids=true | all-gather | bytes 73728 | tf_op jit(solution)/shard_map/all_gather | solution.py:81
  167.0 64.7 %pad_maximum_fusion.10 = (f32[2048,4096]{1,0:T(8,128)}, f32[2304,4096]{1,0:T(8,128)}, f32[2048,4096]{1,0:T(8,128)}) fusion(f32[128,4096]{1,0:T(8,128)} %collective-permute-done, f32[2048,4096]{1,0:T(8,128)} %param.5, f32[2304,4096]{1,0:T(8,128)} %constant_dynamic-update-slice_fusion.2, f32[128,4096]{1,0:T(8,128)S(1)} %collective-permute-done.1), kind=kLoop, calls=%fused_computation.68 | loop fusion | flops 16777216 | bytes 138412032 | tf_op jit(solution)/shard_map/concatenate | solution.py:16
  231.7 3.2 constant_dynamic-update-slice_fusion
  236.6 21.5 %collective-permute-start.2 = (f32[2304,128]{1,0:T(8,128)S(1)}, f32[2304,128]{1,0:T(8,128)S(1)}, u32[]{:S(2)}, u32[]{:S(2)}) collective-permute-start(f32[2304,128]{1,0:T(8,128)S(1)} %get-tuple-element.7), channel_id=1, source_target_pairs={{0,1},{1,2},{2,3},{4,5},{5,6},{6,7},{8,9},{9,10},{10,11},{12,13},{... | collective-permute-start | bytes 3538952 | tf_op jit(solution)/shard_map/ppermute | solution.py:18
  260.4 112.2 %fusion.6 = f32[16,128,4096]{2,1,0:T(8,128)} fusion(f32[18,128,4096]{2,1,0:T(8,128)} %bitcast.85, f32[16,128,4096]{2,1,0:T(8,128)} %bitcast.92, f32[16,128,4096]{2,1,0:T(8,128)} %bitcast.91, f32[16,128,4096]{2,1,0:T(8,128)} %bitcast.84, f32[16,128]{1,0:T(8,128)S(1)} %get-tuple-element.19, f32[16,128]{1,0:T(8,128)S(1)} %get-tuple-element.20, ...), kind=kLoop, calls=%fused_computation.25 | loop fusion | flops 142606336 | bytes 172040192 | tf_op jit(solution)/shard_map/add | solution.py:52
  372.6 28.0 %pad_maximum_fusion.5 = f32[2048,4352]{1,0:T(8,128)} fusion(f32[2304,128]{1,0:T(8,128)S(1)} %collective-permute-done.3, f32[2304,4096]{1,0:T(8,128)} %constant_dynamic-update-slice_fusion, f32[2304,128]{1,0:T(8,128)S(1)} %collective-permute-done.2), kind=kLoop, calls=%fused_computation.5 | loop fusion | flops 17825792 | bytes 75759616 | tf_op jit(solution)/shard_map/concatenate | solution.py:16
  400.5 35.8 %copy.19 = f32[2048,4352]{0,1:T(8,128)} copy(f32[2048,4352]{1,0:T(8,128)} %pad_maximum_fusion.5) | data formatting | bytes 71303168 | tf_op jit(solution)/shard_map/slice | solution.py:71
  436.4 121.7 %fusion.38 = f32[2048,32,128]{0,2,1:T(8,128)} fusion(f32[2048,34,128]{0,2,1:T(8,128)} %bitcast.83, f32[32,128]{1,0:T(8,128)S(1)} %get-tuple-element.28, f32[32,128]{1,0:T(8,128)S(1)} %get-tuple-element.29, f32[32,128]{1,0:T(8,128)S(1)} %get-tuple-element.30, f32[32,128]{1,0:T(8,128)S(1)} %get-tuple-element.31, f32[32,128]{1,0:T(8,128)S(1)} %get-tuple-element.32, ...), kind=kLoop, calls=%fused_computation.63 | loop fusion | flops 142606336 | bytes 170016768 | tf_op jit(solution)/shard_map/add | solution.py:63
  558.1 31.2 %copy.20 = f32[2048,4096]{1,0:T(8,128)} copy(f32[2048,4096]{0,1:T(8,128)} %bitcast.90) | data formatting | bytes 67108864 | tf_op jit(solution)/shard_map/reshape | solution.py:73
  589.3 53.9 %multiply_add_fusion = f32[2048,4096]{1,0:T(8,128)} fusion(f32[2048,4096]{1,0:T(8,128)} %param.5, f32[2048,4096]{1,0:T(8,128)} %param.6, f32[2048,4096]{1,0:T(8,128)} %copy.20, f32[16,128,4096]{2,1,0:T(8,128)} %fusion.6), kind=kLoop, calls=%fused_computation.82 | loop fusion | flops 33554432 | bytes 167772160 | tf_op jit(solution)/shard_map/add | solution.py:100
  647.7 3.3 collective-permute-start.5
  651.0 87.1 %collective-permute-done.4 = f32[128,4096]{1,0:T(8,128)S(1)} collective-permute-done((f32[128,4096]{1,0:T(8,128)S(1)}, f32[128,4096]{1,0:T(8,128)S(1)}, u32[]{:S(2)}, u32[]{:S(2)}) %collective-permute-start.4) | collective-permute-done | bytes 2097184 | tf_op jit(solution)/shard_map/ppermute | solution.py:20
  738.1 25.3 %pad_maximum_fusion = f32[2304,4096]{1,0:T(8,128)} fusion(f32[128,4096]{1,0:T(8,128)S(1)} %collective-permute-done.4, f32[2048,4096]{1,0:T(8,128)} %multiply_add_fusion, f32[128,4096]{1,0:T(8,128)} %collective-permute-done.5), kind=kLoop, calls=%fused_computation | loop fusion | flops 18874368 | bytes 75497472 | tf_op jit(solution)/shard_map/concatenate | solution.py:16
  765.2 4.5 collective-permute-start.6
  772.1 41.7 %pad_maximum_fusion.8 = (f32[2048,4096]{1,0:T(8,128)}, f32[2048,4096]{1,0:T(8,128)}) fusion(f32[128,4096]{1,0:T(8,128)S(1)} %collective-permute-done.4, f32[2048,4096]{1,0:T(8,128)} %multiply_add_fusion, f32[128,4096]{1,0:T(8,128)} %collective-permute-done.5), kind=kLoop, calls=%fused_computation.55 | loop fusion | flops 16777216 | bytes 104857600 | tf_op jit(solution)/shard_map/concatenate | solution.py:16
  813.8 111.9 %fusion.18 = f32[16,128,4096]{2,1,0:T(8,128)} fusion(f32[18,128,4096]{2,1,0:T(8,128)} %bitcast.86, f32[16,128,4096]{2,1,0:T(8,128)} %bitcast.88, f32[16,128,4096]{2,1,0:T(8,128)} %bitcast.87, f32[16,128,4096]{2,1,0:T(8,128)} %bitcast.81, f32[16,128]{1,0:T(8,128)S(1)} %copy-done.21, f32[16,128]{1,0:T(8,128)S(1)} %copy-done.23, f32[16,128]{1,0:T(8,128)S(1)} %copy-done.25, ...), kind=kLoop, calls=%fused_computation.37 | loop fusion | flops 142606336 | bytes 172040192 | tf_op jit(solution)/shard_map/add | solution.py:52
  925.7 27.9 %pad_maximum_fusion.1 = f32[2048,4352]{1,0:T(8,128)} fusion(f32[2304,128]{1,0:T(8,128)S(1)} %collective-permute-done.7, f32[2304,128]{1,0:T(8,128)S(1)} %collective-permute-done.6, f32[128,4096]{1,0:T(8,128)S(1)} %collective-permute-done.4, f32[2048,4096]{1,0:T(8,128)} %multiply_add_fusion, f32[128,4096]{1,0:T(8,128)} %collective-permute-done.5), kind=kLoop, calls=%fused_computation.1 | loop fusion | flops 35651584 | bytes 75759616 | tf_op jit(solution)/shard_map/concatenate | solution.py:16
  953.7 35.8 %copy.21 = f32[2048,4352]{0,1:T(8,128)} copy(f32[2048,4352]{1,0:T(8,128)} %pad_maximum_fusion.1) | data formatting | bytes 71303168 | tf_op jit(solution)/shard_map/slice | solution.py:71
  989.6 121.7 %fusion.30 = f32[2048,32,128]{0,2,1:T(8,128)} fusion(f32[2048,34,128]{0,2,1:T(8,128)} %bitcast.82, f32[32,128]{1,0:T(8,128)S(1)} %copy-done.3, f32[32,128]{1,0:T(8,128)S(1)} %copy-done.5, f32[32,128]{1,0:T(8,128)S(1)} %copy-done.7, f32[32,128]{1,0:T(8,128)S(1)} %copy-done.9, f32[32,128]{1,0:T(8,128)S(1)} %copy-done.11, f32[32,128]{1,0:T(8,128)S(1)} %copy-done.13, ...), kind=kLoop, calls=%fused_computation.50 | loop fusion | flops 142606336 | bytes 170016768 | tf_op jit(solution)/shard_map/add | solution.py:63
  1111.3 31.2 %copy.22 = f32[2048,4096]{1,0:T(8,128)} copy(f32[2048,4096]{0,1:T(8,128)} %bitcast.89) | data formatting | bytes 67108864 | tf_op jit(solution)/shard_map/reshape | solution.py:73
  1142.5 74.2 %fusion.43 = f32[2048,4096]{1,0:T(8,128)} fusion(f32[2048,4096]{1,0:T(8,128)} %param.5, f32[2048,4096]{1,0:T(8,128)} %param.6, f32[2048,4096]{1,0:T(8,128)} %copy.22, f32[16,128,4096]{2,1,0:T(8,128)} %fusion.18, f32[2048,4096]{1,0:T(8,128)} %copy.20, f32[16,128,4096]{2,1,0:T(8,128)} %fusion.6), kind=kLoop, calls=%fused_computation.73 | loop fusion | flops 58720256 | bytes 234881024 | tf_op jit(solution)/shard_map/add | solution.py:102
  (99 shorter events, 20.5 us)
Async XLA Ops:
  4.7 160.8 %collective-permute-start.1 = (f32[128,4096]{1,0:T(8,128)}, f32[128,4096]{1,0:T(8,128)S(1)}, u32[]{:S(2)}, u32[]{:S(2)}) collective-permute-start(f32[128,4096]{1,0:T(8,128)} %get-tuple-element.17), channel_id=1, source_target_pairs={{0,4},{4,8},{8,12},{12,16},{16,20},{20,24},{24,28},{1,5},{5,9},{9,... | collective-permute-start | bytes 6291464 | tf_op jit(solution)/shard_map/ppermute | solution.py:18
  7.8 159.2 %collective-permute-start = (f32[128,4096]{1,0:T(8,128)}, f32[128,4096]{1,0:T(8,128)}, u32[]{:S(2)}, u32[]{:S(2)}) collective-permute-start(f32[128,4096]{1,0:T(8,128)} %get-tuple-element.16), channel_id=1, source_target_pairs={{4,0},{8,4},{12,8},{16,12},{20,16},{24,20},{28,24},{5,1},{9,5},{13... | collective-permute-start | bytes 6291464 | tf_op jit(solution)/shard_map/ppermute | solution.py:20
  165.2 95.1 %copy-start.18 = (f32[16,128]{1,0:T(8,128)}, f32[16,128]{1,0:T(8,128)S(1)}, u32[]{:S(2)}) copy-start(f32[16,128]{1,0:T(8,128)S(1)} %get-tuple-element.18) | copy-start | bytes 24580
  165.2 95.1 %copy-start.20 = (f32[16,128]{1,0:T(8,128)}, f32[16,128]{1,0:T(8,128)S(1)}, u32[]{:S(2)}) copy-start(f32[16,128]{1,0:T(8,128)S(1)} %get-tuple-element.19) | copy-start | bytes 24580
  165.3 95.1 %copy-start.22 = (f32[16,128]{1,0:T(8,128)}, f32[16,128]{1,0:T(8,128)S(1)}, u32[]{:S(2)}) copy-start(f32[16,128]{1,0:T(8,128)S(1)} %get-tuple-element.20) | copy-start | bytes 24580
  165.3 95.1 %copy-start.24 = (f32[16,128]{1,0:T(8,128)}, f32[16,128]{1,0:T(8,128)S(1)}, u32[]{:S(2)}) copy-start(f32[16,128]{1,0:T(8,128)S(1)} %get-tuple-element.21) | copy-start | bytes 24580
  165.3 95.1 %copy-start.26 = (f32[16,128]{1,0:T(8,128)}, f32[16,128]{1,0:T(8,128)S(1)}, u32[]{:S(2)}) copy-start(f32[16,128]{1,0:T(8,128)S(1)} %get-tuple-element.22) | copy-start | bytes 24580
  165.3 95.1 %copy-start.28 = (f32[16,128]{1,0:T(8,128)}, f32[16,128]{1,0:T(8,128)S(1)}, u32[]{:S(2)}) copy-start(f32[16,128]{1,0:T(8,128)S(1)} %get-tuple-element.23) | copy-start | bytes 24580
  165.3 95.1 %copy-start.30 = (f32[16,128]{1,0:T(8,128)}, f32[16,128]{1,0:T(8,128)S(1)}, u32[]{:S(2)}) copy-start(f32[16,128]{1,0:T(8,128)S(1)} %get-tuple-element.24) | copy-start | bytes 24580
  165.4 270.9 %copy-start = (f32[32,128]{1,0:T(8,128)}, f32[32,128]{1,0:T(8,128)S(1)}, u32[]{:S(2)}) copy-start(f32[32,128]{1,0:T(8,128)S(1)} %get-tuple-element.27) | copy-start | bytes 49156
  165.4 270.9 %copy-start.2 = (f32[32,128]{1,0:T(8,128)}, f32[32,128]{1,0:T(8,128)S(1)}, u32[]{:S(2)}) copy-start(f32[32,128]{1,0:T(8,128)S(1)} %get-tuple-element.28) | copy-start | bytes 49156
  165.4 270.9 %copy-start.4 = (f32[32,128]{1,0:T(8,128)}, f32[32,128]{1,0:T(8,128)S(1)}, u32[]{:S(2)}) copy-start(f32[32,128]{1,0:T(8,128)S(1)} %get-tuple-element.29) | copy-start | bytes 49156
  165.4 270.9 %copy-start.6 = (f32[32,128]{1,0:T(8,128)}, f32[32,128]{1,0:T(8,128)S(1)}, u32[]{:S(2)}) copy-start(f32[32,128]{1,0:T(8,128)S(1)} %get-tuple-element.30) | copy-start | bytes 49156
  165.4 270.9 %copy-start.8 = (f32[32,128]{1,0:T(8,128)}, f32[32,128]{1,0:T(8,128)S(1)}, u32[]{:S(2)}) copy-start(f32[32,128]{1,0:T(8,128)S(1)} %get-tuple-element.31) | copy-start | bytes 49156
  165.4 270.9 %copy-start.10 = (f32[32,128]{1,0:T(8,128)}, f32[32,128]{1,0:T(8,128)S(1)}, u32[]{:S(2)}) copy-start(f32[32,128]{1,0:T(8,128)S(1)} %get-tuple-element.32) | copy-start | bytes 49156
  165.4 270.9 %copy-start.12 = (f32[32,128]{1,0:T(8,128)}, f32[32,128]{1,0:T(8,128)S(1)}, u32[]{:S(2)}) copy-start(f32[32,128]{1,0:T(8,128)S(1)} %get-tuple-element.33) | copy-start | bytes 49156
  165.5 270.9 %copy-start.14 = (f32[32,128]{1,0:T(8,128)}, f32[32,128]{1,0:T(8,128)S(1)}, u32[]{:S(2)}) copy-start(f32[32,128]{1,0:T(8,128)S(1)} %get-tuple-element.34) | copy-start | bytes 49156
  165.5 270.9 %copy-start.16 = (f32[32,128]{1,0:T(8,128)}, f32[32,128]{1,0:T(8,128)S(1)}, u32[]{:S(2)}) copy-start(f32[32,128]{1,0:T(8,128)S(1)} %get-tuple-element.35) | copy-start | bytes 49156
  236.6 135.9 %collective-permute-start.2 = (f32[2304,128]{1,0:T(8,128)S(1)}, f32[2304,128]{1,0:T(8,128)S(1)}, u32[]{:S(2)}, u32[]{:S(2)}) collective-permute-start(f32[2304,128]{1,0:T(8,128)S(1)} %get-tuple-element.7), channel_id=1, source_target_pairs={{0,1},{1,2},{2,3},{4,5},{5,6},{6,7},{8,9},{9,10},{10,11},{12,13},{... | collective-permute-start | bytes 3538952 | tf_op jit(solution)/shard_map/ppermute | solution.py:18
  258.2 114.4 %collective-permute-start.3 = (f32[2304,128]{1,0:T(8,128)S(1)}, f32[2304,128]{1,0:T(8,128)S(1)}, u32[]{:S(2)}, u32[]{:S(2)}) collective-permute-start(f32[2304,128]{1,0:T(8,128)S(1)} %get-tuple-element.8), channel_id=1, source_target_pairs={{1,0},{2,1},{3,2},{5,4},{6,5},{7,6},{9,8},{10,9},{11,10},{13,12},{... | collective-permute-start | bytes 3538952 | tf_op jit(solution)/shard_map/ppermute | solution.py:20
  645.7 92.4 %collective-permute-start.4 = (f32[128,4096]{1,0:T(8,128)S(1)}, f32[128,4096]{1,0:T(8,128)S(1)}, u32[]{:S(2)}, u32[]{:S(2)}) collective-permute-start(f32[128,4096]{1,0:T(8,128)S(1)} %get-tuple-element.12), channel_id=1, source_target_pairs={{4,0},{8,4},{12,8},{16,12},{20,16},{24,20},{28,24},{5,1},{9,5},{13... | collective-permute-start | bytes 6291464 | tf_op jit(solution)/shard_map/ppermute | solution.py:20
  647.7 90.4 %collective-permute-start.5 = (f32[128,4096]{1,0:T(8,128)S(1)}, f32[128,4096]{1,0:T(8,128)}, u32[]{:S(2)}, u32[]{:S(2)}) collective-permute-start(f32[128,4096]{1,0:T(8,128)S(1)} %get-tuple-element.11), channel_id=1, source_target_pairs={{0,4},{4,8},{8,12},{12,16},{16,20},{20,24},{24,28},{1,5},{5,9},{9,... | collective-permute-start | bytes 6291464 | tf_op jit(solution)/shard_map/ppermute | solution.py:18
  765.2 160.5 %collective-permute-start.6 = (f32[2304,128]{1,0:T(8,128)S(1)}, f32[2304,128]{1,0:T(8,128)S(1)}, u32[]{:S(2)}, u32[]{:S(2)}) collective-permute-start(f32[2304,128]{1,0:T(8,128)S(1)} %get-tuple-element.5), channel_id=1, source_target_pairs={{0,1},{1,2},{2,3},{4,5},{5,6},{6,7},{8,9},{9,10},{10,11},{12,13},{... | collective-permute-start | bytes 3538952 | tf_op jit(solution)/shard_map/ppermute | solution.py:18
  769.8 155.9 %collective-permute-start.7 = (f32[2304,128]{1,0:T(8,128)S(1)}, f32[2304,128]{1,0:T(8,128)S(1)}, u32[]{:S(2)}, u32[]{:S(2)}) collective-permute-start(f32[2304,128]{1,0:T(8,128)S(1)} %get-tuple-element.6), channel_id=1, source_target_pairs={{1,0},{2,1},{3,2},{5,4},{6,5},{7,6},{9,8},{10,9},{11,10},{13,12},{... | collective-permute-start | bytes 3538952 | tf_op jit(solution)/shard_map/ppermute | solution.py:20
  (20 other events, 909.5 us)
where the time goes:
time: 1220 us
  other arithmetic  783 us (64%)
  blocking collectives  154 us (13%)
  local copies, waits for them, and re-layouts  150 us (12%)
  waiting for transfers between devices  87.1 us (7%)
  starting transfers between devices  41.9 us (3%)
    add x2, other arithmetic, col_term(): total = total + weights[index][None, :, :] * piece  243 us
    add x2, other arithmetic, row_term(): total = total + weights[index][:, :, None] * piece  224 us
    concatenate x5, other arithmetic, padded_2(): jnp.concatenate([lax.ppermute(tail, axis, [(i, (i + 1) % count) for i in...  187 us
    all_gather x1, blocking collectives, per_device(): lax.all_gather(diffusivity, 'row', axis=0, tiled=True)  105 us
    ppermute x4, waiting for transfers between devices, padded_2(): lax.ppermute(head, axis, [((i + 1) % count, i) for i in range(ends)])  87.1 us
    add x1, other arithmetic, per_device(): return cov + 0.5 * time_step * (first + second)  74.2 us
    slice x2, local copies, waits for them, and re-layouts, derive(): padded[side:side + rows, :].reshape(rows, cols // side + 2, side)  71.6 us
    reshape x2, local copies, waits for them, and re-layouts, derive(): along_cols = col_term(middle_rows, col_weights).reshape(rows, cols)  62.4 us
  transfers between devices with their start and end apart: 8, of which 1 were waited for; matrix products, arithmetic and copies ran while one was open for 22% of the time, Pallas kernels for 0%

commit v1 on v0

v1 whole, which is shorter than its diff:
```python
import functools
import jax
import jax.numpy as jnp
from jax import lax
from jax.experimental import pallas as pl
from jax.experimental.pallas import tpu as pltpu
from jax.sharding import PartitionSpec as P

time_step = 0.1
BOTH = ("row", "col")
BAND = 2


def term_weights(kappa, flow_x, flow_y):
    a = kappa / 6.0
    b = 0.5 * flow_y
    c = 0.5 * flow_x

    def later(v):
        return jnp.pad(v[:, 1:], ((0, 0), (0, 1)))

    def earlier(v):
        return jnp.pad(v[:, :-1], ((0, 0), (1, 0)))

    return jnp.stack(
        [later(a), later(4.0 * a + b), earlier(a), earlier(4.0 * a - b), 4.0 * a + c, 4.0 * a - c, -20.0 * a]
    )


def stencil_kernel(side, scale, up_ref, x_ref, dn_ref, base_ref, rw_ref, cw_ref, o_ref):
    step = pl.program_id(0)
    has_up = (step > 0).astype(jnp.float32)
    has_dn = (step < pl.num_programs(0) - 1).astype(jnp.float32)
    band = x_ref.shape[0] // side
    blocks = x_ref.shape[1] // side

    def block(j, first, last):
        here = pl.ds(pl.multiple_of(j * side, side), side)
        cw = [cw_ref[m : m + 1, here] for m in range(7)]
        for x in range(band):
            rows = slice(x * side, (x + 1) * side)
            rw = [rw_ref[m, rows, :] for m in range(7)]
            mid = x_ref[rows, here]
            up = up_ref[:, here] * has_up if x == 0 else x_ref[(x - 1) * side : x * side, here]
            dn = dn_ref[:, here] * has_dn if x == band - 1 else x_ref[(x + 1) * side : (x + 2) * side, here]
            both = up + dn
            acc = pltpu.roll(rw[0] * both + rw[1] * mid, 1, 0)
            acc = acc + pltpu.roll(rw[2] * both + rw[3] * mid, side - 1, 0)
            acc = acc + (rw[4] * up + rw[5] * dn)
            acc = acc + (rw[6] + cw[6]) * mid
            if scale:
                acc = acc + (base_ref[rows, here] + scale * mid)
            else:
                acc = acc + base_ref[rows, here]
            if not first:
                left = x_ref[rows, pl.ds(pl.multiple_of((j - 1) * side, side), side)]
            if not last:
                right = x_ref[rows, pl.ds(pl.multiple_of((j + 1) * side, side), side)]
            if first:
                both = right
                acc = acc + cw[5] * right
            elif last:
                both = left
                acc = acc + cw[4] * left
            else:
                both = left + right
                acc = acc + (cw[4] * left + cw[5] * right)
            acc = acc + pltpu.roll(cw[0] * both + cw[1] * mid, 1, 1)
            acc = acc + pltpu.roll(cw[2] * both + cw[3] * mid, side - 1, 1)
            o_ref[rows, here] = acc

    block(0, True, False)

    @pl.loop(1, blocks - 1)
    def _(j):
        block(j, False, False)

    block(blocks - 1, False, True)


def local_stencil(field, base, row_w, col_w, side, scale):
    rows, cols = field.shape
    steps = rows // (BAND * side)
    lines = rows // side
    tall = (BAND * side, cols)
    return pl.pallas_call(
        functools.partial(stencil_kernel, side, scale),
        grid=(steps,),
        out_shape=jax.ShapeDtypeStruct((rows, cols), jnp.float32),
        in_specs=[
            pl.BlockSpec((side, cols), lambda i: (jnp.maximum(i * BAND - 1, 0), 0)),
            pl.BlockSpec(tall, lambda i: (i, 0)),
            pl.BlockSpec((side, cols), lambda i: (jnp.minimum(i * BAND + BAND, lines - 1), 0)),
            pl.BlockSpec(tall, lambda i: (i, 0)),
            pl.BlockSpec((7, BAND * side, side), lambda i: (0, i, 0)),
            pl.BlockSpec((8, cols), lambda i: (0, 0)),
        ],
        out_specs=pl.BlockSpec(tall, lambda i: (i, 0)),
        compiler_params=pltpu.CompilerParams(
            dimension_semantics=("arbitrary",), vmem_limit_bytes=50 * 1024 * 1024
        ),
        cost_estimate=pl.CostEstimate(
            flops=34 * rows * cols, bytes_accessed=16 * rows * cols, transcendentals=0
        ),
    )(field, field, field, base, row_w, col_w)


def column_weights(cells, row_axis, col_axis):
    nrow, ncol = lax.axis_size(row_axis), lax.axis_size(col_axis)
    if nrow % ncol:
        every = lax.all_gather(cells, row_axis, axis=1, tiled=True)
        count = every.shape[1] // ncol
        return lax.dynamic_slice_in_dim(every, lax.axis_index(col_axis) * count, count, 1)
    ratio = nrow // ncol
    turn = lax.axis_index(row_axis) // ncol
    parts = []
    for e in range(ratio):
        mine = None
        for f in range(ratio):
            perm = [
                ((ratio * c + e) * ncol + d, (f * ncol + d) * ncol + c) for c in range(ncol) for d in range(ncol)
            ]
            got = lax.ppermute(cells, BOTH, perm)
            mine = got if mine is None else mine + got
        parts.append(mine)
    return jnp.concatenate(parts, axis=1)


def row_halos(field, side):
    nrow, ncol = lax.axis_size("row"), lax.axis_size("col")
    rows, cols = field.shape
    ends = nrow - 1
    if nrow != 2 * ncol:
        above = lax.ppermute(field[rows - side :], "row", [(i, i + 1) for i in range(ends)])
        below = lax.ppermute(field[:side], "row", [(i + 1, i) for i in range(ends)])
        return above, below
    half = cols // 2
    parity = lax.axis_index("row") % 2
    odd = parity == 1
    start = parity * half
    lines = rows // side

    def flat(r, c):
        return r * ncol + c

    def slab(at_even, at_odd):
        at = jnp.where(odd, at_odd * side, at_even * side)
        return lax.dynamic_slice(field, (0, at), (rows, side)).T

    turned_above = lax.ppermute(
        slab(2 * lines - 1, lines - 1),
        BOTH,
        [(flat(2 * c + r % 2, (r - 1) // 2), flat(r, c)) for r in range(1, nrow) for c in range(ncol)],
    )
    turned_below = lax.ppermute(
        slab(lines, 0),
        BOTH,
        [(flat(2 * c + r % 2, (r + 1) // 2), flat(r, c)) for r in range(ends) for c in range(ncol)],
    )
    above = lax.ppermute(
        lax.dynamic_slice(field, (rows - side, start), (side, half)), "row", [(i, i + 1) for i in range(ends)]
    )
    below = lax.ppermute(
        lax.dynamic_slice(field, (0, start), (side, half)), "row", [(i + 1, i) for i in range(ends)]
    )

    def joined(turned, plain):
        return jnp.concatenate([jnp.where(odd, plain, turned), jnp.where(odd, turned, plain)], axis=1)

    return joined(turned_above, above), joined(turned_below, below)


def col_halos(field, side):
    ends = lax.axis_size("col") - 1
    cols = field.shape[1]
    left = lax.ppermute(field[:, cols - side :], "col", [(i, i + 1) for i in range(ends)])
    right = lax.ppermute(field[:, :side], "col", [(i + 1, i) for i in range(ends)])
    return left, right


def corrected(total, halos, row_w, col_w, side):
    (above, below), (left, right) = halos
    rows, cols = total.shape

    def down(v):
        return jnp.pad(v[:-1], ((1, 0), (0, 0)))

    def up(v):
        return jnp.pad(v[1:], ((0, 1), (0, 0)))

    def lanes_on(v):
        return jnp.pad(v[:, :-1], ((0, 0), (1, 0)))

    def lanes_back(v):
        return jnp.pad(v[:, 1:], ((0, 0), (0, 1)))

    def of_row(halo, line, centre):
        w = [row_w[m, line][:, None] for m in range(7)]
        return down(w[0] * halo) + up(w[2] * halo) + w[centre] * halo

    def of_col(halo, line, centre):
        w = [col_w[m, line][None, :] for m in range(7)]
        return lanes_on(w[0] * halo) + lanes_back(w[2] * halo) + w[centre] * halo

    def added(total, piece, at):
        old = lax.slice(total, at, (at[0] + piece.shape[0], at[1] + piece.shape[1]))
        return lax.dynamic_update_slice(total, old + piece, at)

    total = added(total, of_col(left, 0, 4), (0, 0))
    total = added(total, of_col(right, -1, 5), (0, cols - side))
    total = added(total, of_row(above, 0, 4), (0, 0))
    return added(total, of_row(below, -1, 5), (rows - side, 0))


def per_device(cov, noise, diffusivity, wind_x, wind_y):
    side = diffusivity.shape[1]
    rows, cols = cov.shape
    cells = jnp.stack([diffusivity, wind_x, wind_y])
    row_w = term_weights(*cells)
    col_w = term_weights(*column_weights(cells, "row", "col"))

    def kernel_weights(scale):
        wide = jnp.broadcast_to((scale * row_w).reshape(7, rows, 1), (7, rows, side))
        return wide, jnp.pad((scale * col_w).reshape(7, cols), ((0, 1), (0, 0)))

    halos = row_halos(cov, side), col_halos(cov, side)
    first = local_stencil(cov, noise, *kernel_weights(1.0), side, None)
    first = corrected(first, halos, row_w, col_w, side)
    halos = row_halos(first, side), col_halos(first, side)
    scale = 0.5 * time_step * time_step
    out = local_stencil(first, cov, *kernel_weights(scale), side, time_step)
    return corrected(out, halos, scale * row_w, scale * col_w, side)


def solution(mesh):
    return jax.shard_map(
        per_device,
        mesh=mesh,
        in_specs=(P("row", "col"), P("row", "col"), P("row", None), P("row", None), P("row", None)),
        out_specs=P("row", "col"),
        check_vma=False,
    )
```

time: 1220 us -> 406 us (0.33)
  other arithmetic: 783 us -> 37.4 us
  blocking collectives: 154 us -> 0 us
  Pallas kernels: 0 us -> 125 us
  waiting for transfers between devices: 87.1 us -> 8.72 us
  local copies, waits for them, and re-layouts: 150 us -> 172 us
  starting transfers between devices: 41.9 us -> 57.5 us
    add x6 -> x3, other arithmetic: 596 us -> 3.59 us  [the longest x1 3.58 us: added(): return lax.dynamic_update_slice(total, old + piece, at)]
    concatenate x5 -> x0, other arithmetic: 187 us -> none  [padded_2(): jnp.concatenate([lax.ppermute(tail, axis, [(i, (i + 1) % count) for i in...]
    all_gather x3 -> x0, blocking collectives: 154 us -> none  [the longest x1 105 us: per_device(): lax.all_gather(diffusivity, 'row', axis=0, tiled=True)]
    pallas_call x0 -> x2, Pallas kernels: none -> 125 us  [local_stencil(): pl.pallas_call(functools.partial(stencil_kernel, side, scale), grid=(step...]
    slice x6 -> x11, local copies, waits for them, and re-layouts: 82.4 us -> 1.93 us  [the longest x4 1.43 us: up(): return jnp.pad(v[1:], ((0, 1), (0, 0)))]
    ppermute x8 -> x16, waiting for transfers between devices: 87.1 us -> 8.72 us  [the longest x2 4.42 us: col_halos(): lax.ppermute(field[:, cols - side:], 'col', [(i, i + 1) for i in range(en...]
    pallas_call x0 -> x2, local copies, waits for them, and re-layouts: none -> 66.8 us  [local_stencil(): pl.pallas_call(functools.partial(stencil_kernel, side, scale), grid=(step...]
    dynamic_update_slice x0 -> x3, local copies, waits for them, and re-layouts: none -> 63.6 us  [added(): return lax.dynamic_update_slice(total, old + piece, at)]
  transfers between devices with their start and end apart: 8 -> 16, of which waited for: 1 -> 2; matrix products, arithmetic and copies ran while one was open for 22% -> 37% of each run, Pallas kernels for 0% -> 31%
where the time goes in v1:
time: 406 us; the launch traced here: 401 us
  local copies, waits for them, and re-layouts  172 us (42%)
  Pallas kernels  125 us (31%)
  starting transfers between devices  57.5 us (14%)
  other arithmetic  37.4 us (9%)
  waiting for transfers between devices  8.72 us (2%)
    pallas_call x2, Pallas kernels, local_stencil(): pl.pallas_call(functools.partial(stencil_kernel, side, scale), grid=(step...  125 us
    pallas_call x2, local copies, waits for them, and re-layouts, local_stencil(): pl.pallas_call(functools.partial(stencil_kernel, side, scale), grid=(step...  66.8 us
    dynamic_update_slice x3, local copies, waits for them, and re-layouts, added(): return lax.dynamic_update_slice(total, old + piece, at)  63.6 us
    dynamic_update_slice x7, other arithmetic, added(): return lax.dynamic_update_slice(total, old + piece, at)  21.4 us
    unnamed x42, local copies, waits for them, and re-layouts  13.9 us
    ppermute x2, starting transfers between devices, row_halos(): lax.ppermute(lax.dynamic_slice(field, (rows - side, start), (side, half))...  13 us
    ppermute x2, starting transfers between devices, row_halos(): lax.ppermute(slab(lines, 0), BOTH, [(flat(2 * c + r % 2, (r + 1) // 2), f...  11.1 us
    ppermute x2, starting transfers between devices, row_halos(): lax.ppermute(slab(2 * lines - 1, lines - 1), BOTH, [(flat(2 * c + r % 2,...  9.2 us
  transfers between devices with their start and end apart: 16, of which 2 were waited for; matrix products, arithmetic and copies ran while one was open for 37% of the time, Pallas kernels for 31%

profile of v1, /device:TPU:9, one launch (start us, length us, event | category | flops | bytes accessed | tf_op | source)
XLA Modules:
  0.0 401.1 jit_solution(18103859943305435019)
XLA Ops:
  0.7 3.0 collective-permute-start
  7.5 3.8 dynamic-slice_bitcast_fusion.2
  12.7 6.5 %collective-permute-start.4 = (f32[2048,128]{0,1:T(8,128)}, f32[2048,128]{0,1:T(8,128)S(1)}, u32[]{:S(2)}, u32[]{:S(2)}) collective-permute-start(f32[2048,128]{0,1:T(8,128)} %copy.28), channel_id=1, source_target_pairs={{0,1},{1,2},{2,3},{4,5},{5,6},{6,7},{8,9},{9,10},{10,11},{12,13},{... | collective-permute-start | bytes 3145736 | tf_op jit(solution)/shard_map/ppermute | solution.py:176
  33.0 3.7 collective-permute-start.6
  36.7 5.4 %collective-permute-start.7 = (f32[128,2048]{0,1:T(8,128)}, f32[128,2048]{0,1:T(8,128)}, u32[]{:S(2)}, u32[]{:S(2)}) collective-permute-start(f32[128,2048]{0,1:T(8,128)} %get-tuple-element.26), channel_id=1, source_target_pairs={{4,4},{12,5},{20,6},{28,7},{0,8},{8,9},{16,10},{24,11},{5,12},{13,... | collective-permute-start | bytes 3145736 | tf_op jit(solution)/shard_map/ppermute | solution.py:150
  42.2 2.8 collective-permute-start.8
  45.7 4.2 %broadcast_in_dim.13.rw_ref = f32[7,2048,128]{2,1,0:T(8,128)} broadcast(f32[7,2048]{1,0:T(8,128)S(1)} %bitcast.136), dimensions={0,1} | broadcast | bytes 7397376 | tf_op jit(solution)/shard_map/broadcast_in_dim | solution.py:223
  49.9 61.5 %shard_map.55 = f32[2048,4096]{1,0:T(8,128)} custom-call(f32[2048,4096]{1,0:T(8,128)} %base_ref.3, f32[2048,4096]{1,0:T(8,128)} %base_ref.3, f32[2048,4096]{1,0:T(8,128)} %base_ref.3, f32[2048,4096]{1,0:T(8,128)} %base_ref.2, f32[7,2048,128]{2,1,0:T(8,128)} %broadcast_in_dim.13.rw_ref, f32[8,4096]{1,0:T(8,128)S(1)} %pad.95.cw_ref), custom_call_target="tpu_custom_call" | custom-call | flops 285212672 | bytes 134217728 | tf_op jit(solution)/shard_map/pallas_call | solution.py:86
  111.4 33.5 %copy.15 = f32[2048,4096]{0,1:T(8,128)} copy(f32[2048,4096]{1,0:T(8,128)} %shard_map.55) | data formatting | bytes 67108864 | tf_op jit(solution)/shard_map/pallas_call | solution.py:86
  154.7 3.6 fusion.30
  158.4 31.1 %copy.19 = f32[2048,4096]{1,0:T(8,128)} copy(f32[2048,4096]{0,1:T(8,128)} %fusion.30) | data formatting | bytes 67108864 | tf_op jit(solution)/shard_map/dynamic_update_slice | solution.py:207
  191.8 3.6 fusion.22
  198.8 3.8 dynamic-slice_bitcast_fusion
  205.3 9.5 %collective-permute-start.15 = (f32[128,2048]{0,1:T(8,128)}, f32[128,2048]{0,1:T(8,128)}, u32[]{:S(2)}, u32[]{:S(2)}) collective-permute-start(f32[128,2048]{0,1:T(8,128)} %get-tuple-element.17), channel_id=1, source_target_pairs={{0,0},{8,1},{16,2},{24,3},{5,4},{13,5},{21,6},{29,7},{1,8},{9,9},{... | collective-permute-start | bytes 3145736 | tf_op jit(solution)/shard_map/ppermute | solution.py:155
  219.3 3.8 collective-permute-start.13
  224.5 9.3 %collective-permute-start.12 = (f32[128,2048]{0,1:T(8,128)}, f32[128,2048]{0,1:T(8,128)S(1)}, u32[]{:S(2)}, u32[]{:S(2)}) collective-permute-start(f32[128,2048]{0,1:T(8,128)} %copy.34), channel_id=1, source_target_pairs={{0,4},{4,8},{8,12},{12,16},{16,20},{20,24},{24,28},{1,5},{5,9},{9,... | collective-permute-start | bytes 3145736 | tf_op jit(solution)/shard_map/ppermute | solution.py:160
  235.4 4.2 %broadcast_in_dim.14.rw_ref = f32[7,2048,128]{2,1,0:T(8,128)} broadcast(f32[7,2048]{1,0:T(8,128)S(1)} %broadcast_multiply_fusion.2), dimensions={0,1} | broadcast | bytes 7397376 | tf_op jit(solution)/shard_map/broadcast_in_dim | solution.py:223
  239.6 63.4 %shard_map.56 = f32[2048,4096]{1,0:T(8,128)} custom-call(f32[2048,4096]{1,0:T(8,128)} %constant_dynamic-update-slice_fusion.14.up_ref.x_ref.dn_ref, f32[2048,4096]{1,0:T(8,128)} %constant_dynamic-update-slice_fusion.14.up_ref.x_ref.dn_ref, f32[2048,4096]{1,0:T(8,128)} %constant_dynamic-update-slice_fusion.14.up_ref.x_ref.dn_ref, f32[2048,4096]{1,0:T(8,128)} %base_ref.3, ...), custom_call_target="tpu_custom_call" | custom-call | flops 285212672 | bytes 134217728 | tf_op jit(solution)/shard_map/pallas_call | solution.py:86
  303.0 33.4 %copy.23 = f32[2048,4096]{0,1:T(8,128)} copy(f32[2048,4096]{1,0:T(8,128)} %shard_map.56) | data formatting | bytes 67108864 | tf_op jit(solution)/shard_map/pallas_call | solution.py:86
  347.2 4.4 %collective-permute-done.10 = f32[2048,128]{0,1:T(8,128)S(1)} collective-permute-done((f32[2048,128]{0,1:T(8,128)}, f32[2048,128]{0,1:T(8,128)S(1)}, u32[]{:S(2)}, u32[]{:S(2)}) %collective-permute-start.10) | collective-permute-done | bytes 1048608 | tf_op jit(solution)/shard_map/ppermute | solution.py:176
  353.0 4.3 %collective-permute-done.11 = f32[2048,128]{0,1:T(8,128)S(1)} collective-permute-done((f32[2048,128]{0,1:T(8,128)}, f32[2048,128]{0,1:T(8,128)S(1)}, u32[]{:S(2)}, u32[]{:S(2)}) %collective-permute-start.11) | collective-permute-done | bytes 1048608 | tf_op jit(solution)/shard_map/ppermute | solution.py:177
  362.7 3.6 fusion.15
  366.4 3.6 fusion.7
  370.0 31.1 %copy.27 = f32[2048,4096]{1,0:T(8,128)} copy(f32[2048,4096]{0,1:T(8,128)} %fusion.7) | data formatting | bytes 67108864 | tf_op jit(solution)/shard_map/dynamic_update_slice | solution.py:207
  (134 shorter events, 63.5 us)
Async XLA Ops:
  0.7 30.3 %collective-permute-start = (f32[3,16,128]{2,1,0:T(8,128)S(1)}, f32[3,16,128]{2,1,0:T(8,128)S(1)}, u32[]{:S(2)}, u32[]{:S(2)}) collective-permute-start(f32[3,16,128]{2,1,0:T(8,128)S(1)} %pad_maximum_fusion.4), channel_id=1, source_target_pairs={{0,0},{1,4},{2,8},{3,12},{8,1},{9,5},{10,9},{11,13},{16,2},{17,6},... | collective-permute-start | bytes 73736 | tf_op jit(solution)/shard_map/ppermute | solution.py:123
  3.7 29.2 %collective-permute-start.1 = (f32[3,16,128]{2,1,0:T(8,128)S(1)}, f32[3,16,128]{2,1,0:T(8,128)S(1)}, u32[]{:S(2)}, u32[]{:S(2)}) collective-permute-start(f32[3,16,128]{2,1,0:T(8,128)S(1)} %pad_maximum_fusion.4), channel_id=1, source_target_pairs={{0,16},{1,20},{2,24},{3,28},{8,17},{9,21},{10,25},{11,29},{16,18},... | collective-permute-start | bytes 73736 | tf_op jit(solution)/shard_map/ppermute | solution.py:123
  5.5 31.2 %collective-permute-start.2 = (f32[3,16,128]{2,1,0:T(8,128)S(1)}, f32[3,16,128]{2,1,0:T(8,128)S(1)}, u32[]{:S(2)}, u32[]{:S(2)}) collective-permute-start(f32[3,16,128]{2,1,0:T(8,128)S(1)} %pad_maximum_fusion.4), channel_id=1, source_target_pairs={{4,0},{5,4},{6,8},{7,12},{12,1},{13,5},{14,9},{15,13},{20,2},{21,6... | collective-permute-start | bytes 73736 | tf_op jit(solution)/shard_map/ppermute | solution.py:123
  6.8 35.3 %collective-permute-start.3 = (f32[3,16,128]{2,1,0:T(8,128)S(1)}, f32[3,16,128]{2,1,0:T(8,128)S(1)}, u32[]{:S(2)}, u32[]{:S(2)}) collective-permute-start(f32[3,16,128]{2,1,0:T(8,128)S(1)} %pad_maximum_fusion.4), channel_id=1, source_target_pairs={{4,16},{5,20},{6,24},{7,28},{12,17},{13,21},{14,25},{15,29},{20,18... | collective-permute-start | bytes 73736 | tf_op jit(solution)/shard_map/ppermute | solution.py:123
  11.4 7.9 %copy-start.1 = (f32[16,128]{1,0:T(8,128)S(1)}, f32[16,128]{1,0:T(8,128)}, u32[]{:S(2)}) copy-start(f32[16,128]{1,0:T(8,128)} %param.7) | copy-start | bytes 24580
  11.4 7.9 %copy-start.4 = (f32[16,128]{1,0:T(8,128)S(1)}, f32[16,128]{1,0:T(8,128)}, u32[]{:S(2)}) copy-start(f32[16,128]{1,0:T(8,128)} %param.9) | copy-start | bytes 24580
  11.4 8.4 %copy-start.3 = (f32[16,128]{1,0:T(8,128)S(1)}, f32[16,128]{1,0:T(8,128)}, u32[]{:S(2)}) copy-start(f32[16,128]{1,0:T(8,128)} %param.8) | copy-start | bytes 24580
  12.7 135.7 %collective-permute-start.4 = (f32[2048,128]{0,1:T(8,128)}, f32[2048,128]{0,1:T(8,128)S(1)}, u32[]{:S(2)}, u32[]{:S(2)}) collective-permute-start(f32[2048,128]{0,1:T(8,128)} %copy.28), channel_id=1, source_target_pairs={{0,1},{1,2},{2,3},{4,5},{5,6},{6,7},{8,9},{9,10},{10,11},{12,13},{... | collective-permute-start | bytes 3145736 | tf_op jit(solution)/shard_map/ppermute | solution.py:176
  31.0 118.2 %collective-permute-start.5 = (f32[2048,128]{0,1:T(8,128)}, f32[2048,128]{0,1:T(8,128)S(1)}, u32[]{:S(2)}, u32[]{:S(2)}) collective-permute-start(f32[2048,128]{0,1:T(8,128)} %copy.29), channel_id=1, source_target_pairs={{1,0},{2,1},{3,2},{5,4},{6,5},{7,6},{9,8},{10,9},{11,10},{13,12},{... | collective-permute-start | bytes 3145736 | tf_op jit(solution)/shard_map/ppermute | solution.py:177
  33.0 112.1 %collective-permute-start.6 = (f32[128,2048]{0,1:T(8,128)}, f32[128,2048]{0,1:T(8,128)}, u32[]{:S(2)}, u32[]{:S(2)}) collective-permute-start(f32[128,2048]{0,1:T(8,128)} %copy.30), channel_id=1, source_target_pairs={{0,4},{4,8},{8,12},{12,16},{16,20},{20,24},{24,28},{1,5},{5,9},{9,... | collective-permute-start | bytes 3145736 | tf_op jit(solution)/shard_map/ppermute | solution.py:160
  36.7 110.0 %collective-permute-start.7 = (f32[128,2048]{0,1:T(8,128)}, f32[128,2048]{0,1:T(8,128)}, u32[]{:S(2)}, u32[]{:S(2)}) collective-permute-start(f32[128,2048]{0,1:T(8,128)} %get-tuple-element.26), channel_id=1, source_target_pairs={{4,4},{12,5},{20,6},{28,7},{0,8},{8,9},{16,10},{24,11},{5,12},{13,... | collective-permute-start | bytes 3145736 | tf_op jit(solution)/shard_map/ppermute | solution.py:150
  42.2 147.3 %collective-permute-start.8 = (f32[128,2048]{0,1:T(8,128)}, f32[128,2048]{0,1:T(8,128)}, u32[]{:S(2)}, u32[]{:S(2)}) collective-permute-start(f32[128,2048]{0,1:T(8,128)} %copy.31), channel_id=1, source_target_pairs={{4,0},{8,4},{12,8},{16,12},{20,16},{24,20},{28,24},{5,1},{9,5},{13... | collective-permute-start | bytes 3145736 | tf_op jit(solution)/shard_map/ppermute | solution.py:163
  45.4 4.5 %copy-start.2 = (f32[7,32,128]{2,1,0:T(8,128)}, f32[7,32,128]{2,1,0:T(8,128)S(1)}, u32[]{:S(2)}) copy-start(f32[7,32,128]{2,1,0:T(8,128)S(1)} %get-tuple-element.9) | copy-start | bytes 344068
  111.4 33.6 %copy-start = (f32[128,2048]{0,1:T(8,128)S(1)}, f32[128,2048]{0,1:T(8,128)}, u32[]{:S(2)}) copy-start(f32[128,2048]{0,1:T(8,128)} %get-tuple-element.23) | copy-start | bytes 3145732
  145.0 44.4 %collective-permute-start.9 = (f32[128,2048]{0,1:T(8,128)S(1)}, f32[128,2048]{0,1:T(8,128)}, u32[]{:S(2)}, u32[]{:S(2)}) collective-permute-start(f32[128,2048]{0,1:T(8,128)S(1)} %copy-done), channel_id=1, source_target_pairs={{0,0},{8,1},{16,2},{24,3},{5,4},{13,5},{21,6},{29,7},{1,8},{9,9},{... | collective-permute-start | bytes 3145736 | tf_op jit(solution)/shard_map/ppermute | solution.py:155
  152.1 2.6 copy-start.12
  205.3 135.6 %collective-permute-start.15 = (f32[128,2048]{0,1:T(8,128)}, f32[128,2048]{0,1:T(8,128)}, u32[]{:S(2)}, u32[]{:S(2)}) collective-permute-start(f32[128,2048]{0,1:T(8,128)} %get-tuple-element.17), channel_id=1, source_target_pairs={{0,0},{8,1},{16,2},{24,3},{5,4},{13,5},{21,6},{29,7},{1,8},{9,9},{... | collective-permute-start | bytes 3145736 | tf_op jit(solution)/shard_map/ppermute | solution.py:155
  217.4 126.0 %collective-permute-start.14 = (f32[128,2048]{0,1:T(8,128)}, f32[128,2048]{0,1:T(8,128)}, u32[]{:S(2)}, u32[]{:S(2)}) collective-permute-start(f32[128,2048]{0,1:T(8,128)} %copy.35), channel_id=1, source_target_pairs={{4,0},{8,4},{12,8},{16,12},{20,16},{24,20},{28,24},{5,1},{9,5},{13... | collective-permute-start | bytes 3145736 | tf_op jit(solution)/shard_map/ppermute | solution.py:163
  219.3 125.8 %collective-permute-start.13 = (f32[128,2048]{0,1:T(8,128)}, f32[128,2048]{0,1:T(8,128)}, u32[]{:S(2)}, u32[]{:S(2)}) collective-permute-start(f32[128,2048]{0,1:T(8,128)} %get-tuple-element.20), channel_id=1, source_target_pairs={{4,4},{12,5},{20,6},{28,7},{0,8},{8,9},{16,10},{24,11},{5,12},{13,... | collective-permute-start | bytes 3145736 | tf_op jit(solution)/shard_map/ppermute | solution.py:150
  224.5 120.7 %collective-permute-start.12 = (f32[128,2048]{0,1:T(8,128)}, f32[128,2048]{0,1:T(8,128)S(1)}, u32[]{:S(2)}, u32[]{:S(2)}) collective-permute-start(f32[128,2048]{0,1:T(8,128)} %copy.34), channel_id=1, source_target_pairs={{0,4},{4,8},{8,12},{12,16},{16,20},{20,24},{24,28},{1,5},{5,9},{9,... | collective-permute-start | bytes 3145736 | tf_op jit(solution)/shard_map/ppermute | solution.py:160
  337.7 14.0 %collective-permute-start.10 = (f32[2048,128]{0,1:T(8,128)}, f32[2048,128]{0,1:T(8,128)S(1)}, u32[]{:S(2)}, u32[]{:S(2)}) collective-permute-start(f32[2048,128]{0,1:T(8,128)} %copy.32), channel_id=1, source_target_pairs={{0,1},{1,2},{2,3},{4,5},{5,6},{6,7},{8,9},{9,10},{10,11},{12,13},{... | collective-permute-start | bytes 3145736 | tf_op jit(solution)/shard_map/ppermute | solution.py:176
  340.9 16.3 %collective-permute-start.11 = (f32[2048,128]{0,1:T(8,128)}, f32[2048,128]{0,1:T(8,128)S(1)}, u32[]{:S(2)}, u32[]{:S(2)}) collective-permute-start(f32[2048,128]{0,1:T(8,128)} %copy.33), channel_id=1, source_target_pairs={{1,0},{2,1},{3,2},{5,4},{6,5},{7,6},{9,8},{10,9},{11,10},{13,12},{... | collective-permute-start | bytes 3145736 | tf_op jit(solution)/shard_map/ppermute | solution.py:177
  360.1 2.6 copy-start.8
  362.7 3.7 copy-start.7
  (5 other events, 4.8 us)

commit v2 on v1

v2 whole, which is shorter than its diff:
```python
import functools
import jax
import jax.numpy as jnp
from jax import lax
from jax.experimental import pallas as pl
from jax.experimental.pallas import tpu as pltpu
from jax.sharding import PartitionSpec as P

time_step = 0.1
BOTH = ("row", "col")
second_scale = 0.5 * time_step * time_step
BAND = 2


def term_weights(kappa, flow_x, flow_y):
    a = kappa / 6.0
    b = 0.5 * flow_y
    c = 0.5 * flow_x

    def later(v):
        return jnp.pad(v[:, 1:], ((0, 0), (0, 1)))

    def earlier(v):
        return jnp.pad(v[:, :-1], ((0, 0), (1, 0)))

    return jnp.stack(
        [later(a), later(4.0 * a + b), earlier(a), earlier(4.0 * a - b), 4.0 * a + c, 4.0 * a - c, -20.0 * a]
    )


def stencil_kernel(side, first_stage, x_ref, dn_ref, base_ref, rw_ref, cw_ref, o_ref, carry):
    step = pl.program_id(0)
    has_dn = (step < pl.num_programs(0) - 1).astype(jnp.float32)
    band = x_ref.shape[0] // side
    blocks = x_ref.shape[1] // side

    @pl.when(step == 0)
    def _():
        carry[...] = jnp.zeros_like(carry)

    def block(j, first, last):
        here = pl.ds(pl.multiple_of(j * side, side), side)
        cw = [cw_ref[m : m + 1, here] for m in range(7)]
        for x in range(band):
            rows = slice(x * side, (x + 1) * side)
            rw = [rw_ref[m, rows, :] for m in range(7)]
            mid = x_ref[rows, here]
            up = carry[:, here] if x == 0 else x_ref[(x - 1) * side : x * side, here]
            dn = dn_ref[:, here] * has_dn if x == band - 1 else x_ref[(x + 1) * side : (x + 2) * side, here]
            both = up + dn
            acc = pltpu.roll(rw[0] * both + rw[1] * mid, 1, 0)
            acc = acc + pltpu.roll(rw[2] * both + rw[3] * mid, side - 1, 0)
            acc = acc + (rw[4] * up + rw[5] * dn)
            acc = acc + (rw[6] + cw[6]) * mid
            if not first:
                left = x_ref[rows, pl.ds(pl.multiple_of((j - 1) * side, side), side)]
            if not last:
                right = x_ref[rows, pl.ds(pl.multiple_of((j + 1) * side, side), side)]
            if first:
                both = right
                acc = acc + cw[5] * right
            elif last:
                both = left
                acc = acc + cw[4] * left
            else:
                both = left + right
                acc = acc + (cw[4] * left + cw[5] * right)
            acc = acc + pltpu.roll(cw[0] * both + cw[1] * mid, 1, 1)
            acc = acc + pltpu.roll(cw[2] * both + cw[3] * mid, side - 1, 1)
            if first_stage:
                o_ref[rows, here] = base_ref[rows, here] + acc
            else:
                o_ref[rows, here] = base_ref[rows, here] + (time_step * mid + second_scale * acc)

    block(0, True, False)

    @pl.loop(1, blocks - 1)
    def _(j):
        block(j, False, False)

    block(blocks - 1, False, True)
    carry[...] = x_ref[(band - 1) * side :, :]


def local_stencil(field, base, row_w, col_w, side, first_stage):
    rows, cols = field.shape
    steps = rows // (BAND * side)
    lines = rows // side
    tall = (BAND * side, cols)
    return pl.pallas_call(
        functools.partial(stencil_kernel, side, first_stage),
        grid=(steps,),
        out_shape=jax.ShapeDtypeStruct((rows, cols), jnp.float32),
        in_specs=[
            pl.BlockSpec(tall, lambda i: (i, 0)),
            pl.BlockSpec((side, cols), lambda i: (jnp.minimum(i * BAND + BAND, lines - 1), 0)),
            pl.BlockSpec(tall, lambda i: (i, 0)),
            pl.BlockSpec((7, BAND * side, side), lambda i: (0, i, 0)),
            pl.BlockSpec((8, cols), lambda i: (0, 0)),
        ],
        out_specs=pl.BlockSpec(tall, lambda i: (i, 0)),
        scratch_shapes=[pltpu.VMEM((side, cols), jnp.float32)],
        compiler_params=pltpu.CompilerParams(
            dimension_semantics=("arbitrary",), vmem_limit_bytes=48 * 1024 * 1024
        ),
        cost_estimate=pl.CostEstimate(
            flops=34 * rows * cols, bytes_accessed=14 * rows * cols, transcendentals=0
        ),
    )(field, field, base, row_w, col_w)


def column_weights(cells, row_axis, col_axis):
    nrow, ncol = lax.axis_size(row_axis), lax.axis_size(col_axis)
    if nrow % ncol:
        every = lax.all_gather(cells, row_axis, axis=1, tiled=True)
        count = every.shape[1] // ncol
        return lax.dynamic_slice_in_dim(every, lax.axis_index(col_axis) * count, count, 1)
    ratio = nrow // ncol
    turn = lax.axis_index(row_axis) // ncol
    parts = []
    for e in range(ratio):
        mine = None
        for f in range(ratio):
            perm = [
                ((ratio * c + e) * ncol + d, (f * ncol + d) * ncol + c) for c in range(ncol) for d in range(ncol)
            ]
            got = lax.ppermute(cells, BOTH, perm)
            mine = got if mine is None else mine + got
        parts.append(mine)
    return jnp.concatenate(parts, axis=1)


def pack_kernel(places, above_t, below_t, top, bottom, head, tail, *outs):
    outs[0][...] = above_t[...].T
    outs[1][...] = below_t[...].T
    for piece, out in zip((top, bottom, head, tail), outs[2:]):
        out[...] = piece[...]


def packed(field, side):
    rows, cols = field.shape
    lines, blocks = rows // side, cols // side
    chunk = min(4 * side, rows)
    steps = rows // chunk
    parity = lax.axis_index("row") % 2
    odd = parity == 1
    places = jnp.stack([jnp.where(odd, lines - 1, 2 * lines - 1), jnp.where(odd, 0, lines), parity]).astype(jnp.int32)
    tall, wide = (chunk, side), (side, chunk)
    laid = jax.ShapeDtypeStruct((side, rows), jnp.float32)
    stood = jax.ShapeDtypeStruct((rows, side), jnp.float32)
    return pl.pallas_call(
        pack_kernel,
        grid_spec=pltpu.PrefetchScalarGridSpec(
            num_scalar_prefetch=1,
            grid=(steps,),
            in_specs=[
                pl.BlockSpec(tall, lambda i, p: (i, p[0])),
                pl.BlockSpec(tall, lambda i, p: (i, p[1])),
                pl.BlockSpec(wide, lambda i, p: (0, p[2] * steps + i)),
                pl.BlockSpec(wide, lambda i, p: (lines - 1, p[2] * steps + i)),
                pl.BlockSpec(tall, lambda i, p: (i, 0)),
                pl.BlockSpec(tall, lambda i, p: (i, blocks - 1)),
            ],
            out_specs=[pl.BlockSpec(wide, lambda i, p: (0, i))] * 4 + [pl.BlockSpec(tall, lambda i, p: (i, 0))] * 2,
        ),
        out_shape=[laid] * 4 + [stood] * 2,
        compiler_params=pltpu.CompilerParams(vmem_limit_bytes=40 * 1024 * 1024),
        cost_estimate=pl.CostEstimate(flops=0, bytes_accessed=48 * side * rows, transcendentals=0),
    )(places, *[field] * 6)


def halos_of(field, side):
    nrow, ncol = lax.axis_size("row"), lax.axis_size("col")
    rows, cols = field.shape
    ends, half = nrow - 1, cols // 2
    onward = [(i, i + 1) for i in range(ends)]
    back = [(i + 1, i) for i in range(ends)]
    col_onward = [(i, i + 1) for i in range(ncol - 1)]
    col_back = [(i + 1, i) for i in range(ncol - 1)]
    if nrow != 2 * ncol:
        above = lax.ppermute(field[rows - side :], "row", onward)
        below = lax.ppermute(field[:side], "row", back)
        left = lax.ppermute(field[:, cols - side :], "col", col_onward)
        right = lax.ppermute(field[:, :side], "col", col_back)
        pick = jnp.zeros((1,), jnp.int32)
        return pick, (above[:, :half], above[:, half:], below[:, :half], below[:, half:]), (left, right)

    def flat(r, c):
        return r * ncol + c

    to_below = [(flat(2 * c + r % 2, (r - 1) // 2), flat(r, c)) for r in range(1, nrow) for c in range(ncol)]
    to_above = [(flat(2 * c + r % 2, (r + 1) // 2), flat(r, c)) for r in range(ends) for c in range(ncol)]
    above_t, below_t, top, bottom, head, tail = packed(field, side)
    above = lax.ppermute(bottom, "row", onward)
    below = lax.ppermute(top, "row", back)
    above_t = lax.ppermute(above_t, BOTH, to_below)
    below_t = lax.ppermute(below_t, BOTH, to_above)
    left = lax.ppermute(tail, "col", col_onward)
    right = lax.ppermute(head, "col", col_back)
    pick = (lax.axis_index("row") % 2).astype(jnp.int32).reshape(1)
    return pick, (above_t, above, below_t, below), (left, right)


def col_edge_kernel(side, scale, total_ref, left_ref, right_ref, cw_ref, o_ref):
    start = pl.program_id(0) == 0
    halo = jnp.where(start, left_ref[...], right_ref[...])
    near = jnp.where(start, cw_ref[4:5, :], cw_ref[5:6, :])
    piece = pltpu.roll(cw_ref[0:1, :] * halo, 1, 1) + pltpu.roll(cw_ref[2:3, :] * halo, side - 1, 1) + near * halo
    o_ref[...] = total_ref[...] + scale * piece


def row_edge_kernel(side, scale, pick, total_ref, a_ref, b_ref, c_ref, d_ref, rw_ref, o_ref):
    start = pl.program_id(0) == 0
    picked = pl.program_id(1) // (pl.num_programs(1) // 2) == pick[0]
    near = jnp.where(start, rw_ref[4], rw_ref[5])
    for j in range(total_ref.shape[1] // side):
        here = slice(j * side, (j + 1) * side)
        above = jnp.where(picked, a_ref[:, here], b_ref[:, here])
        below = jnp.where(picked, c_ref[:, here], d_ref[:, here])
        halo = jnp.where(start, above, below)
        piece = pltpu.roll(rw_ref[0] * halo, 1, 0) + pltpu.roll(rw_ref[2] * halo, side - 1, 0) + near * halo
        o_ref[:, here] = total_ref[:, here] + scale * piece


def corrected(total, halos, row_w, col_w, side, scale):
    pick, row_parts, (left, right) = halos
    rows, cols = total.shape
    lines, blocks = rows // side, cols // side
    chunk = min(4 * side, rows)
    same = jax.ShapeDtypeStruct(total.shape, jnp.float32)
    spot = pl.BlockSpec((chunk, side), lambda s, i: (i, s * (blocks - 1)))
    halo = pl.BlockSpec((chunk, side), lambda s, i: (i, 0))
    total = pl.pallas_call(
        functools.partial(col_edge_kernel, side, scale),
        grid=(2, rows // chunk),
        out_shape=same,
        in_specs=[spot, halo, halo, pl.BlockSpec((8, side), lambda s, i: (0, s * (blocks - 1)))],
        out_specs=spot,
        input_output_aliases={0: 0},
        compiler_params=pltpu.CompilerParams(vmem_limit_bytes=40 * 1024 * 1024),
        cost_estimate=pl.CostEstimate(flops=14 * side * rows, bytes_accessed=32 * side * rows, transcendentals=0),
    )(total, left, right, col_w)
    chunk = min(4 * side, cols // 2)
    steps = cols // chunk
    spot = pl.BlockSpec((side, chunk), lambda s, j, p: (s * (lines - 1), j))
    halo = pl.BlockSpec((side, chunk), lambda s, j, p: (0, j % (steps // 2)))
    return pl.pallas_call(
        functools.partial(row_edge_kernel, side, scale),
        grid_spec=pltpu.PrefetchScalarGridSpec(
            num_scalar_prefetch=1,
            grid=(2, steps),
            in_specs=[spot] + [halo] * 4 + [pl.BlockSpec((7, side, side), lambda s, j, p: (0, s * (lines - 1), 0))],
            out_specs=spot,
        ),
        out_shape=same,
        input_output_aliases={1: 0},
        compiler_params=pltpu.CompilerParams(vmem_limit_bytes=40 * 1024 * 1024),
        cost_estimate=pl.CostEstimate(flops=14 * side * cols, bytes_accessed=40 * side * cols, transcendentals=0),
    )(pick, total, *row_parts, row_w)


def per_device(cov, noise, diffusivity, wind_x, wind_y):
    side = diffusivity.shape[1]
    rows, cols = cov.shape
    cells = jnp.stack([diffusivity, wind_x, wind_y])
    row_w = jnp.broadcast_to(term_weights(*cells).reshape(7, rows, 1), (7, rows, side))
    col_w = jnp.pad(term_weights(*column_weights(cells, "row", "col")).reshape(7, cols), ((0, 1), (0, 0)))
    weights = row_w, col_w, side

    halos = halos_of(cov, side)
    first = corrected(local_stencil(cov, noise, *weights, True), halos, *weights, 1.0)
    halos = halos_of(first, side)
    return corrected(local_stencil(first, cov, *weights, False), halos, *weights, second_scale)


def solution(mesh):
    return jax.shard_map(
        per_device,
        mesh=mesh,
        in_specs=(P("row", "col"), P("row", "col"), P("row", None), P("row", None), P("row", None)),
        out_specs=P("row", "col"),
        check_vma=False,
    )
```

time: 406 us -> 259 us (0.64)
  local copies, waits for them, and re-layouts: 172 us -> 4.96 us
  Pallas kernels: 125 us -> 177 us
  other arithmetic: 37.4 us -> 0.19 us
  waiting for transfers between devices: 8.72 us -> 20.1 us
  starting transfers between devices: 57.5 us -> 53.1 us
    pallas_call x2 -> x0, local copies, waits for them, and re-layouts: 66.8 us -> none  [local_stencil(): pl.pallas_call(functools.partial(stencil_kernel, side, scale), grid=(step...]
    dynamic_update_slice x3 -> x0, local copies, waits for them, and re-layouts: 63.6 us -> none  [added(): return lax.dynamic_update_slice(total, old + piece, at)]
    pallas_call x2 -> x8, Pallas kernels: 125 us -> 177 us  [the longest x2 127 us: local_stencil(): pl.pallas_call(functools.partial(stencil_kernel, side, first_stage), grid...]
    dynamic_update_slice x7 -> x0, other arithmetic: 21.4 us -> none  [added(): return lax.dynamic_update_slice(total, old + piece, at)]
    unnamed x42 -> x12, local copies, waits for them, and re-layouts: 13.9 us -> 0.02 us
    ppermute x12, waiting for transfers between devices: 8.71 us -> 20.1 us  [the longest x2 20.1 us: halos_of(): left = lax.ppermute(tail, 'col', col_onward)]
    ppermute x12, starting transfers between devices: 50.8 us -> 40.1 us  [the longest x2 10.2 us: halos_of(): below_t = lax.ppermute(below_t, BOTH, to_above)]
    transpose x2 -> x0, local copies, waits for them, and re-layouts: 7.67 us -> none  [slab(): return lax.dynamic_slice(field, (0, at), (rows, side)).T]
  transfers between devices with their start and end apart: 16 -> 16, of which waited for: 2 -> 1; matrix products, arithmetic and copies ran while one was open for 37% -> 2% of each run, Pallas kernels for 31% -> 55%
where the time goes in v2:
time: 259 us; the launch traced here: 256 us
  Pallas kernels  177 us (68%)
  starting transfers between devices  53.1 us (21%)
  waiting for transfers between devices  20.1 us (8%)
  local copies, waits for them, and re-layouts  4.96 us (2%)
    pallas_call x2, Pallas kernels, local_stencil(): pl.pallas_call(functools.partial(stencil_kernel, side, first_stage), grid...  127 us
    pallas_call x2, Pallas kernels, corrected(): pl.pallas_call(functools.partial(row_edge_kernel, side, scale), grid_spec...  24.2 us
    ppermute x2, waiting for transfers between devices, halos_of(): left = lax.ppermute(tail, 'col', col_onward)  20.1 us
    pallas_call x2, Pallas kernels, corrected(): pl.pallas_call(functools.partial(col_edge_kernel, side, scale), grid=(2,...  13.6 us
    ppermute x4, starting transfers between devices, column_weights(): got = lax.ppermute(cells, BOTH, perm)  13 us
    pallas_call x2, Pallas kernels, packed(): pl.pallas_call(pack_kernel, grid_spec=pltpu.PrefetchScalarGridSpec(num_sc...  12.3 us
    ppermute x2, starting transfers between devices, halos_of(): below_t = lax.ppermute(below_t, BOTH, to_above)  10.2 us
    ppermute x2, starting transfers between devices, halos_of(): above_t = lax.ppermute(above_t, BOTH, to_below)  10.1 us
  transfers between devices with their start and end apart: 16, of which 1 were waited for; matrix products, arithmetic and copies ran while one was open for 2% of the time, Pallas kernels for 55%

profile of v2, /device:TPU:9, one launch (start us, length us, event | category | flops | bytes accessed | tf_op | source)
XLA Modules:
  0.0 255.8 jit_solution(758797343339282561)
XLA Ops:
  0.1 6.2 %shard_map.56 = (f32[128,2048]{1,0:T(8,128)}, f32[128,2048]{1,0:T(8,128)}, f32[128,2048]{1,0:T(8,128)}, f32[128,2048]{1,0:T(8,128)}, f32[2048,128]{1,0:T(8,128)}, /*index=5*/f32[2048,128]{1,0:T(8,128)S(1)}) custom-call(s32[3]{0:T(128)S(1)} %pad_add_fusion.places, f32[2048,4096]{1,0:T(8,128)} %base_ref.3, f32[2048,4096]{1,0:T(8,128)} %base_ref.3, ...), custom_call_target="tpu_custom_call" | custom-call | bytes 12582912 | tf_op jit(solution)/shard_map/pallas_call | solution.py:151
  6.3 3.7 %collective-permute-start.4 = (f32[2048,128]{1,0:T(8,128)S(1)}, f32[2048,128]{1,0:T(8,128)S(1)}, u32[]{:S(2)}, u32[]{:S(2)}) collective-permute-start(f32[2048,128]{1,0:T(8,128)S(1)} %get-tuple-element.17), channel_id=1, source_target_pairs={{0,1},{1,2},{2,3},{4,5},{5,6},{6,7},{8,9},{9,10},{10,11},{12,13},{... | collective-permute-start | bytes 3145736 | tf_op jit(solution)/shard_map/ppermute | solution.py:198
  10.7 1.3 collective-permute-start.2
  12.0 9.2 %collective-permute-start.1 = (f32[3,16,128]{2,1,0:T(8,128)S(1)}, f32[3,16,128]{2,1,0:T(8,128)S(1)}, u32[]{:S(2)}, u32[]{:S(2)}) collective-permute-start(f32[3,16,128]{2,1,0:T(8,128)S(1)} %pad_maximum_fusion), channel_id=1, source_target_pairs={{0,16},{1,20},{2,24},{3,28},{8,17},{9,21},{10,25},{11,29},{16,18},... | collective-permute-start | bytes 73736 | tf_op jit(solution)/shard_map/ppermute | solution.py:127
  21.2 1.9 collective-permute-start
  23.2 1.9 collective-permute-start.5
  25.1 1.9 collective-permute-start.6
  27.0 1.9 collective-permute-start.7
  29.0 9.5 %collective-permute-start.8 = (f32[128,2048]{1,0:T(8,128)}, f32[128,2048]{1,0:T(8,128)}, u32[]{:S(2)}, u32[]{:S(2)}) collective-permute-start(f32[128,2048]{1,0:T(8,128)} %get-tuple-element.21), channel_id=1, source_target_pairs={{0,0},{8,1},{16,2},{24,3},{5,4},{13,5},{21,6},{29,7},{1,8},{9,9},{... | collective-permute-start | bytes 3145736 | tf_op jit(solution)/shard_map/ppermute | solution.py:197
  38.4 1.9 collective-permute-start.9
  41.4 4.1 %broadcast_in_dim.8.rw_ref = f32[7,2048,128]{2,1,0:T(8,128)} broadcast(f32[7,2048]{1,0:T(8,128)S(1)} %bitcast.44), dimensions={0,1} | broadcast | bytes 7397376 | tf_op jit(solution)/shard_map/broadcast_in_dim | solution.py:266
  45.5 61.4 %shard_map.55.total_ref = f32[2048,4096]{1,0:T(8,128)} custom-call(f32[2048,4096]{1,0:T(8,128)} %base_ref.3, f32[2048,4096]{1,0:T(8,128)} %base_ref.3, f32[2048,4096]{1,0:T(8,128)} %base_ref.2, f32[7,2048,128]{2,1,0:T(8,128)} %broadcast_in_dim.8.rw_ref, f32[8,4096]{1,0:T(8,128)S(1)} %pad.40.cw_ref), custom_call_target="tpu_custom_call" | custom-call | flops 285212672 | bytes 117440512 | tf_op jit(solution)/shard_map/pallas_call | solution.py:90
  106.9 7.3 %shard_map.57.total_ref = f32[2048,4096]{1,0:T(8,128)} custom-call(f32[2048,4096]{1,0:T(8,128)} %shard_map.55.total_ref, f32[2048,128]{1,0:T(8,128)S(1)} %collective-permute-done.4.left_ref, f32[2048,128]{1,0:T(8,128)} %collective-permute-done.5.right_ref, f32[8,4096]{1,0:T(8,128)S(1)} %pad.40.cw_ref), custom_call_target="tpu_custom_call", output_to_operand_aliasing={{}: (0, {})} | custom-call | flops 3670016 | bytes 8388608 | tf_op jit(solution)/shard_map/pallas_call | solution.py:233
  114.2 12.9 %shard_map.58.x_ref.dn_ref.above_t.below_t.top.bottom.head.tail = f32[2048,4096]{1,0:T(8,128)} custom-call(s32[1]{0:T(128)} %bitcast.pick, f32[2048,4096]{1,0:T(8,128)} %shard_map.57.total_ref, f32[128,2048]{1,0:T(8,128)S(1)} %collective-permute-done.6.a_ref, f32[128,2048]{1,0:T(8,128)S(1)} %collective-permute-done.7.b_ref, ...), custom_call_target="tpu_custom_call", output_to_operand_aliasing={{}: (1, {})} | custom-call | flops 7340032 | bytes 20971520 | tf_op jit(solution)/shard_map/pallas_call | solution.py:247
  127.1 6.1 %shard_map.60 = (f32[128,2048]{1,0:T(8,128)}, f32[128,2048]{1,0:T(8,128)S(1)}, f32[128,2048]{1,0:T(8,128)S(1)}, f32[128,2048]{1,0:T(8,128)}, f32[2048,128]{1,0:T(8,128)}, /*index=5*/f32[2048,128]{1,0:T(8,128)S(1)}) custom-call(s32[3]{0:T(128)S(1)} %pad_add_fusion.places, f32[2048,4096]{1,0:T(8,128)} %shard_map.58.x_ref.dn_ref.above_t.below_t.top.bottom.head.tail, ...), custom_call_target="tpu_custom_call" | custom-call | bytes 12582912 | tf_op jit(solution)/shard_map/pallas_call | solution.py:151
  133.2 1.9 collective-permute-start.10
  135.2 2.5 collective-permute-start.11
  137.6 8.2 %collective-permute-start.12 = (f32[128,2048]{1,0:T(8,128)}, f32[128,2048]{1,0:T(8,128)S(1)}, u32[]{:S(2)}, u32[]{:S(2)}) collective-permute-start(f32[128,2048]{1,0:T(8,128)} %get-tuple-element.25), channel_id=1, source_target_pairs={{4,4},{12,5},{20,6},{28,7},{0,8},{8,9},{16,10},{24,11},{5,12},{13,... | collective-permute-start | bytes 3145736 | tf_op jit(solution)/shard_map/ppermute | solution.py:196
  145.8 3.8 %collective-permute-start.13 = (f32[128,2048]{1,0:T(8,128)}, f32[128,2048]{1,0:T(8,128)S(1)}, u32[]{:S(2)}, u32[]{:S(2)}) collective-permute-start(f32[128,2048]{1,0:T(8,128)} %get-tuple-element.26), channel_id=1, source_target_pairs={{0,4},{4,8},{8,12},{12,16},{16,20},{20,24},{24,28},{1,5},{5,9},{9,... | collective-permute-start | bytes 3145736 | tf_op jit(solution)/shard_map/ppermute | solution.py:194
  150.3 20.1 %collective-permute-done.10.left_ref = f32[2048,128]{1,0:T(8,128)S(1)} collective-permute-done((f32[2048,128]{1,0:T(8,128)S(1)}, f32[2048,128]{1,0:T(8,128)S(1)}, u32[]{:S(2)}, u32[]{:S(2)}) %collective-permute-start.10) | collective-permute-done | bytes 1048608 | tf_op jit(solution)/shard_map/ppermute | solution.py:198
  170.4 2.2 collective-permute-start.15
  172.6 65.6 %shard_map.59.total_ref = f32[2048,4096]{1,0:T(8,128)} custom-call(f32[2048,4096]{1,0:T(8,128)} %shard_map.58.x_ref.dn_ref.above_t.below_t.top.bottom.head.tail, f32[2048,4096]{1,0:T(8,128)} %shard_map.58.x_ref.dn_ref.above_t.below_t.top.bottom.head.tail, f32[2048,4096]{1,0:T(8,128)} %base_ref.3, f32[7,2048,128]{2,1,0:T(8,128)} %broadcast_in_dim.8.rw_ref, ...), custom_call_target="tpu_custom_call" | custom-call | flops 285212672 | bytes 117440512 | tf_op jit(solution)/shard_map/pallas_call | solution.py:90
  238.1 6.3 %shard_map.61.total_ref = f32[2048,4096]{1,0:T(8,128)} custom-call(f32[2048,4096]{1,0:T(8,128)} %shard_map.59.total_ref, f32[2048,128]{1,0:T(8,128)S(1)} %collective-permute-done.10.left_ref, f32[2048,128]{1,0:T(8,128)S(1)} %collective-permute-done.11.right_ref, f32[8,4096]{1,0:T(8,128)S(1)} %pad.40.cw_ref), custom_call_target="tpu_custom_call", output_to_operand_aliasing={{}: (0, {})} | custom-call | flops 3670016 | bytes 8388608 | tf_op jit(solution)/shard_map/pallas_call | solution.py:233
  244.5 11.3 %shard_map.62 = f32[2048,4096]{1,0:T(8,128)} custom-call(s32[1]{0:T(128)} %bitcast.pick, f32[2048,4096]{1,0:T(8,128)} %shard_map.61.total_ref, f32[128,2048]{1,0:T(8,128)S(1)} %collective-permute-done.12.a_ref, f32[128,2048]{1,0:T(8,128)S(1)} %collective-permute-done.13.b_ref, ...), custom_call_target="tpu_custom_call", output_to_operand_aliasing={{}: (1, {})} | custom-call | flops 7340032 | bytes 20971520 | tf_op jit(solution)/shard_map/pallas_call | solution.py:247
  (52 shorter events, 2.5 us)
Async XLA Ops:
  0.1 10.0 %copy-start.1 = (f32[16,128]{1,0:T(8,128)S(1)}, f32[16,128]{1,0:T(8,128)}, u32[]{:S(2)}) copy-start(f32[16,128]{1,0:T(8,128)} %param.8) | copy-start | bytes 24580
  0.1 10.0 %copy-start.2 = (f32[16,128]{1,0:T(8,128)S(1)}, f32[16,128]{1,0:T(8,128)}, u32[]{:S(2)}) copy-start(f32[16,128]{1,0:T(8,128)} %param.7) | copy-start | bytes 24580
  0.1 10.0 %copy-start.3 = (f32[16,128]{1,0:T(8,128)S(1)}, f32[16,128]{1,0:T(8,128)}, u32[]{:S(2)}) copy-start(f32[16,128]{1,0:T(8,128)} %param.9) | copy-start | bytes 24580
  6.3 32.1 %collective-permute-start.4 = (f32[2048,128]{1,0:T(8,128)S(1)}, f32[2048,128]{1,0:T(8,128)S(1)}, u32[]{:S(2)}, u32[]{:S(2)}) collective-permute-start(f32[2048,128]{1,0:T(8,128)S(1)} %get-tuple-element.17), channel_id=1, source_target_pairs={{0,1},{1,2},{2,3},{4,5},{5,6},{6,7},{8,9},{9,10},{10,11},{12,13},{... | collective-permute-start | bytes 3145736 | tf_op jit(solution)/shard_map/ppermute | solution.py:198
  10.1 13.1 %collective-permute-start.3 = (f32[3,16,128]{2,1,0:T(8,128)S(1)}, f32[3,16,128]{2,1,0:T(8,128)S(1)}, u32[]{:S(2)}, u32[]{:S(2)}) collective-permute-start(f32[3,16,128]{2,1,0:T(8,128)S(1)} %pad_maximum_fusion), channel_id=1, source_target_pairs={{4,16},{5,20},{6,24},{7,28},{12,17},{13,21},{14,25},{15,29},{20,18... | collective-permute-start | bytes 73736 | tf_op jit(solution)/shard_map/ppermute | solution.py:127
  10.7 14.3 %collective-permute-start.2 = (f32[3,16,128]{2,1,0:T(8,128)S(1)}, f32[3,16,128]{2,1,0:T(8,128)S(1)}, u32[]{:S(2)}, u32[]{:S(2)}) collective-permute-start(f32[3,16,128]{2,1,0:T(8,128)S(1)} %pad_maximum_fusion), channel_id=1, source_target_pairs={{4,0},{5,4},{6,8},{7,12},{12,1},{13,5},{14,9},{15,13},{20,2},{21,6... | collective-permute-start | bytes 73736 | tf_op jit(solution)/shard_map/ppermute | solution.py:127
  12.0 15.0 %collective-permute-start.1 = (f32[3,16,128]{2,1,0:T(8,128)S(1)}, f32[3,16,128]{2,1,0:T(8,128)S(1)}, u32[]{:S(2)}, u32[]{:S(2)}) collective-permute-start(f32[3,16,128]{2,1,0:T(8,128)S(1)} %pad_maximum_fusion), channel_id=1, source_target_pairs={{0,16},{1,20},{2,24},{3,28},{8,17},{9,21},{10,25},{11,29},{16,18},... | collective-permute-start | bytes 73736 | tf_op jit(solution)/shard_map/ppermute | solution.py:127
  21.2 7.7 %collective-permute-start = (f32[3,16,128]{2,1,0:T(8,128)S(1)}, f32[3,16,128]{2,1,0:T(8,128)S(1)}, u32[]{:S(2)}, u32[]{:S(2)}) collective-permute-start(f32[3,16,128]{2,1,0:T(8,128)S(1)} %pad_maximum_fusion), channel_id=1, source_target_pairs={{0,0},{1,4},{2,8},{3,12},{8,1},{9,5},{10,9},{11,13},{16,2},{17,6},... | collective-permute-start | bytes 73736 | tf_op jit(solution)/shard_map/ppermute | solution.py:127
  23.2 83.7 %collective-permute-start.5 = (f32[2048,128]{1,0:T(8,128)}, f32[2048,128]{1,0:T(8,128)}, u32[]{:S(2)}, u32[]{:S(2)}) collective-permute-start(f32[2048,128]{1,0:T(8,128)} %get-tuple-element.18), channel_id=1, source_target_pairs={{1,0},{2,1},{3,2},{5,4},{6,5},{7,6},{9,8},{10,9},{11,10},{13,12},{... | collective-permute-start | bytes 3145736 | tf_op jit(solution)/shard_map/ppermute | solution.py:199
  25.1 89.0 %collective-permute-start.6 = (f32[128,2048]{1,0:T(8,128)}, f32[128,2048]{1,0:T(8,128)S(1)}, u32[]{:S(2)}, u32[]{:S(2)}) collective-permute-start(f32[128,2048]{1,0:T(8,128)} %get-tuple-element.19), channel_id=1, source_target_pairs={{4,4},{12,5},{20,6},{28,7},{0,8},{8,9},{16,10},{24,11},{5,12},{13,... | collective-permute-start | bytes 3145736 | tf_op jit(solution)/shard_map/ppermute | solution.py:196
  27.0 87.1 %collective-permute-start.7 = (f32[128,2048]{1,0:T(8,128)}, f32[128,2048]{1,0:T(8,128)S(1)}, u32[]{:S(2)}, u32[]{:S(2)}) collective-permute-start(f32[128,2048]{1,0:T(8,128)} %get-tuple-element.20), channel_id=1, source_target_pairs={{0,4},{4,8},{8,12},{12,16},{16,20},{20,24},{24,28},{1,5},{5,9},{9,... | collective-permute-start | bytes 3145736 | tf_op jit(solution)/shard_map/ppermute | solution.py:194
  29.0 85.2 %collective-permute-start.8 = (f32[128,2048]{1,0:T(8,128)}, f32[128,2048]{1,0:T(8,128)}, u32[]{:S(2)}, u32[]{:S(2)}) collective-permute-start(f32[128,2048]{1,0:T(8,128)} %get-tuple-element.21), channel_id=1, source_target_pairs={{0,0},{8,1},{16,2},{24,3},{5,4},{13,5},{21,6},{29,7},{1,8},{9,9},{... | collective-permute-start | bytes 3145736 | tf_op jit(solution)/shard_map/ppermute | solution.py:197
  38.4 75.7 %collective-permute-start.9 = (f32[128,2048]{1,0:T(8,128)}, f32[128,2048]{1,0:T(8,128)}, u32[]{:S(2)}, u32[]{:S(2)}) collective-permute-start(f32[128,2048]{1,0:T(8,128)} %get-tuple-element.22), channel_id=1, source_target_pairs={{4,0},{8,4},{12,8},{16,12},{20,16},{24,20},{28,24},{5,1},{9,5},{13... | collective-permute-start | bytes 3145736 | tf_op jit(solution)/shard_map/ppermute | solution.py:195
  106.8 7.3 %copy-start = (f32[7,2048,128]{2,1,0:T(8,128)S(1)}, f32[7,2048,128]{2,1,0:T(8,128)}, u32[]{:S(2)}) copy-start(f32[7,2048,128]{2,1,0:T(8,128)} %broadcast_in_dim.8.rw_ref) | copy-start | bytes 22020100
  127.1 117.4 %slice-start = ((s8[7340032]{0:T(1024)(128)(4,1)}), s8[4194304]{0:T(1024)(128)(4,1)S(1)}, s32[]{:S(2)}) async-start(s8[7340032]{0:T(1024)(128)(4,1)} %bitcast.42), calls=%async_computation | async-start | bytes 8388608
  133.2 37.2 %collective-permute-start.10 = (f32[2048,128]{1,0:T(8,128)S(1)}, f32[2048,128]{1,0:T(8,128)S(1)}, u32[]{:S(2)}, u32[]{:S(2)}) collective-permute-start(f32[2048,128]{1,0:T(8,128)S(1)} %get-tuple-element.23), channel_id=1, source_target_pairs={{0,1},{1,2},{2,3},{4,5},{5,6},{6,7},{8,9},{9,10},{10,11},{12,13},{... | collective-permute-start | bytes 3145736 | tf_op jit(solution)/shard_map/ppermute | solution.py:198
  135.2 103.0 %collective-permute-start.11 = (f32[2048,128]{1,0:T(8,128)}, f32[2048,128]{1,0:T(8,128)S(1)}, u32[]{:S(2)}, u32[]{:S(2)}) collective-permute-start(f32[2048,128]{1,0:T(8,128)} %get-tuple-element.24), channel_id=1, source_target_pairs={{1,0},{2,1},{3,2},{5,4},{6,5},{7,6},{9,8},{10,9},{11,10},{13,12},{... | collective-permute-start | bytes 3145736 | tf_op jit(solution)/shard_map/ppermute | solution.py:199
  137.6 106.8 %collective-permute-start.12 = (f32[128,2048]{1,0:T(8,128)}, f32[128,2048]{1,0:T(8,128)S(1)}, u32[]{:S(2)}, u32[]{:S(2)}) collective-permute-start(f32[128,2048]{1,0:T(8,128)} %get-tuple-element.25), channel_id=1, source_target_pairs={{4,4},{12,5},{20,6},{28,7},{0,8},{8,9},{16,10},{24,11},{5,12},{13,... | collective-permute-start | bytes 3145736 | tf_op jit(solution)/shard_map/ppermute | solution.py:196
  145.8 98.7 %collective-permute-start.13 = (f32[128,2048]{1,0:T(8,128)}, f32[128,2048]{1,0:T(8,128)S(1)}, u32[]{:S(2)}, u32[]{:S(2)}) collective-permute-start(f32[128,2048]{1,0:T(8,128)} %get-tuple-element.26), channel_id=1, source_target_pairs={{0,4},{4,8},{8,12},{12,16},{16,20},{20,24},{24,28},{1,5},{5,9},{9,... | collective-permute-start | bytes 3145736 | tf_op jit(solution)/shard_map/ppermute | solution.py:194
  149.6 94.9 %collective-permute-start.14 = (f32[128,2048]{1,0:T(8,128)S(1)}, f32[128,2048]{1,0:T(8,128)S(1)}, u32[]{:S(2)}, u32[]{:S(2)}) collective-permute-start(f32[128,2048]{1,0:T(8,128)S(1)} %get-tuple-element.27), channel_id=1, source_target_pairs={{0,0},{8,1},{16,2},{24,3},{5,4},{13,5},{21,6},{29,7},{1,8},{9,9},{... | collective-permute-start | bytes 3145736 | tf_op jit(solution)/shard_map/ppermute | solution.py:197
  170.4 74.1 %slice-start.1 = ((s8[7340032]{0:T(1024)(128)(4,1)}), s8[3145728]{0:T(1024)(128)(4,1)S(1)}, s32[]{:S(2)}) async-start(s8[7340032]{0:T(1024)(128)(4,1)} %bitcast.42), calls=%async_computation.1 | async-start | bytes 6291456
  170.4 74.1 %collective-permute-start.15 = (f32[128,2048]{1,0:T(8,128)S(1)}, f32[128,2048]{1,0:T(8,128)S(1)}, u32[]{:S(2)}, u32[]{:S(2)}) collective-permute-start(f32[128,2048]{1,0:T(8,128)S(1)} %get-tuple-element.28), channel_id=1, source_target_pairs={{4,0},{8,4},{12,8},{16,12},{20,16},{24,20},{28,24},{5,1},{9,5},{13... | collective-permute-start | bytes 3145736 | tf_op jit(solution)/shard_map/ppermute | solution.py:195
